TPU v7x, 512 devices: a whole 4x4x16 slice. The times are simulated.
512 devices in a mesh: leaf: 64 (over z, y), sec: 8 (over x, core).
Axes of the slice: x: 4, y: 4, z: 16, core: 2. Of those that a mesh axis runs over, the one named last changes fastest.
Arguments:
- leaf_inv: bfloat16 [524288, 1024], P(('leaf', 'sec')), may hold values from -0.1875 to 0.1875
- subtree_blocks: int32 [64, 8], P('leaf', 'sec'), may hold values from 1 to 8
- subtree_shift_rhs: bfloat16 [524288, 128], P(('leaf', 'sec')), may hold values from -6 to 6
- leaf_noise: bfloat16 [524288, 128], P(('leaf', 'sec')), may hold values from -6 to 6
- leaf_dev: bfloat16 [524288], P(('leaf', 'sec')), may hold values from 0.29882812 to 3
- sep_inv: bfloat16 [16384, 3584], P(('leaf', 'sec')), may hold values from -0.1875 to 0.1875
- sep_panel: bfloat16 [16384, 3584], P(('leaf', 'sec')), may hold values from -0.1875 to 0.1875
- sep_rhs: bfloat16 [3, 16384, 128], P(None, ('leaf', 'sec')), may hold values from -6 to 6
- sep_noise: bfloat16 [3, 16384, 128], P(None, ('leaf', 'sec')), may hold values from -6 to 6
- sep_dev: bfloat16 [3, 16384], P(None, ('leaf', 'sec')), may hold values from 0.29882812 to 3
Outputs:
- subtree_scaled_samples: bfloat16 [524288, 128], P(('leaf', 'sec'))
- sep_sample: bfloat16 [3, 16384, 128], P(None, ('leaf', 'sec'))
All inputs are finite; a program needn't handle non-finite values.
Results may differ from a plain program's by a relative error of at most 0.019.
Values may be sent and summed in bfloat16 or wider, within the bound.
A program may use at most 64 MiB of HBM per device.

v0:
```python
import jax
import jax.numpy as jnp
from jax import lax
from jax.sharding import PartitionSpec as P

BLOCK = 128


def from_partner(block, axis, apart):
    count = lax.axis_size(axis)
    route = []
    for low in range(count):
        high = low | 1 << apart
        if high != low and high < count:
            route += [(low, high), (high, low)]
    return lax.ppermute(block, axis, route)


def pair_gather(block, height):
    leaf_place = lax.axis_index("leaf")
    for bit_index in range(height):
        partner = from_partner(block, "leaf", bit_index)
        upper_half = leaf_place >> bit_index & 1 == 1
        block = jnp.where(
            upper_half, jnp.concatenate([partner, block], 0), jnp.concatenate([block, partner], 0)
        )
    return block


def group_gather(piece, height):
    block = lax.all_gather(piece, "sec", axis=0, tiled=True)
    return pair_gather(block, height)


def halve_pairs(partial_sum, height):
    leaf_place = lax.axis_index("leaf")
    for bit_index in reversed(range(height)):
        half_rows = partial_sum.shape[0] // 2
        lower_rows = partial_sum[:half_rows]
        upper_rows = partial_sum[half_rows:]
        upper_half = leaf_place >> bit_index & 1 == 1
        kept = jnp.where(upper_half, upper_rows, lower_rows)
        outgoing = jnp.where(upper_half, lower_rows, upper_rows)
        partial_sum = kept + from_partner(outgoing, "leaf", bit_index)
    return partial_sum


def group_reduce(partial_sum, height):
    reduced = halve_pairs(partial_sum, height)
    return lax.psum_scatter(reduced, "sec", scatter_dimension=0, tiled=True)


def transposed_product(matrix, vector):
    return lax.dot_general(
        matrix, vector, (((0,), (0,)), ((), ())), preferred_element_type=jnp.float32
    )


def on_device(
    leaf_inv,
    subtree_blocks,
    subtree_shift_rhs,
    leaf_noise,
    leaf_dev,
    sep_inv,
    sep_panel,
    sep_rhs,
    sep_noise,
    sep_dev,
):
    subtree_row_count = leaf_inv.shape[0]
    row_count = sep_inv.shape[0]
    levels = sep_rhs.shape[0]
    sections = lax.axis_size("sec")
    active_rows = subtree_blocks[0, 0] * BLOCK
    row_positions = jnp.arange(subtree_row_count, dtype=jnp.int32)
    row_activity = (row_positions >= subtree_row_count - active_rows)[:, None]
    subtree_shifted = jnp.where(
        row_activity, subtree_shift_rhs, jnp.zeros((), subtree_shift_rhs.dtype)
    )
    forward_subtree = jnp.dot(leaf_inv, subtree_shifted, preferred_element_type=jnp.float32)
    subtree_forward_solution = jnp.where(row_activity, forward_subtree, jnp.float32(0.0)).astype(
        jnp.bfloat16
    )
    top = subtree_forward_solution[subtree_row_count - row_count :]
    solved = []
    for height in range(1, levels + 1):
        span = 2**height * sections * row_count
        offset = (2**height - 2) * sections * row_count
        children = group_gather(top, height)
        panel = sep_panel[:, offset : offset + span]
        inverse_block = sep_inv[:, offset : offset + span]
        reduced = (
            sep_rhs[height - 1].astype(jnp.float32)
            - jnp.dot(panel, children, preferred_element_type=jnp.float32)
        ).astype(jnp.bfloat16)
        whole_reduced = group_gather(reduced, height)
        result = jnp.dot(inverse_block, whole_reduced, preferred_element_type=jnp.float32).astype(
            jnp.bfloat16
        )
        solved.append(result)
        top = result
    samples = [None] * levels
    correction = None
    for height in range(levels, 0, -1):
        span = 2**height * sections * row_count
        offset = (2**height - 2) * sections * row_count
        panel = sep_panel[:, offset : offset + span]
        inverse_block = sep_inv[:, offset : offset + span]
        summed = solved[height - 1].astype(jnp.float32) + sep_noise[height - 1].astype(jnp.float32)
        if correction is not None:
            summed = summed - correction
        vector = summed.astype(jnp.bfloat16)
        backed = group_reduce(transposed_product(inverse_block, vector), height).astype(
            jnp.bfloat16
        )
        samples[height - 1] = (
            sep_dev[height - 1][:, None].astype(jnp.float32) * backed.astype(jnp.float32)
        ).astype(jnp.bfloat16)
        correction = group_reduce(transposed_product(panel, backed), height)
    leading = jnp.zeros((subtree_row_count - row_count, correction.shape[1]), jnp.float32)
    placed = jnp.concatenate([leading, correction], axis=0)
    subtree_summed = (
        subtree_forward_solution.astype(jnp.float32) + leaf_noise.astype(jnp.float32) - placed
    )
    subtree_weight = jnp.where(row_activity, subtree_summed, jnp.float32(0.0)).astype(jnp.bfloat16)
    subtree_solution = transposed_product(leaf_inv, subtree_weight)
    sample_scales = leaf_dev[:, None].astype(jnp.float32)
    subtree_scaled_samples = jnp.where(
        row_activity, sample_scales * subtree_solution, jnp.float32(0.0)
    ).astype(jnp.bfloat16)
    return (subtree_scaled_samples, jnp.stack(samples))


def solution(mesh):
    in_specs = (
        P(("leaf", "sec"), None),
        P("leaf", "sec"),
        P(("leaf", "sec"), None),
        P(("leaf", "sec"), None),
        P(("leaf", "sec")),
        P(("leaf", "sec"), None),
        P(("leaf", "sec"), None),
        P(None, ("leaf", "sec"), None),
        P(None, ("leaf", "sec"), None),
        P(None, ("leaf", "sec")),
    )
    out_specs = (P(("leaf", "sec"), None), P(None, ("leaf", "sec"), None))
    return jax.shard_map(
        on_device, mesh=mesh, in_specs=in_specs, out_specs=out_specs, check_vma=False
    )
```

profile of v0, /device:TPU:8, one launch (start us, length us, event | category | flops | bytes accessed | tf_op | source)
XLA Modules:
  0.0 543.7 jit_solution(11738488947053809435)
XLA Ops:
  10.1 13.1 %all_gather.18 = bf16[256,128]{1,0:T(8,128)(2,1)S(1)} all-gather(bf16[32,128]{1,0:T(8,128)(2,1)S(1)} %copy.28), channel_id=1, replica_groups=mesh['leaf'=64,'sec'=8] {'sec'}, dimensions={0}, use_global_device_ids=true | all-gather | bytes 73728 | tf_op jit(solution)/shard_map/all_gather | solution.py:31
  23.3 7.4 %collective-permute-start = (bf16[256,128]{1,0:T(8,128)(2,1)S(1)}, bf16[256,128]{1,0:T(8,128)(2,1)S(1)}, u32[]{:S(2)}, u32[]{:S(2)}) collective-permute-start(bf16[256,128]{1,0:T(8,128)(2,1)S(1)} %all_gather.18), channel_id=1, source_target_pairs={{0,8},{8,0},{16,24},{24,16},{32,40},{40,32},{48,56},{56,48},{64,72... | collective-permute-start | bytes 196616 | tf_op jit(solution)/shard_map/ppermute | solution.py:16
  33.3 12.7 %all_gather.19 = bf16[256,128]{1,0:T(8,128)(2,1)S(1)} all-gather(bf16[32,128]{1,0:T(8,128)(2,1)S(1)} %fusion.8), channel_id=1, replica_groups=mesh['leaf'=64,'sec'=8] {'sec'}, dimensions={0}, use_global_device_ids=true | all-gather | bytes 73728 | tf_op jit(solution)/shard_map/all_gather | solution.py:31
  46.1 3.6 collective-permute-start.1
  49.7 2.6 collective-permute-done.1
  53.2 12.7 %all_gather.20 = bf16[256,128]{1,0:T(8,128)(2,1)S(1)} all-gather(bf16[32,128]{1,0:T(8,128)(2,1)S(1)} %fusion.15), channel_id=1, replica_groups=mesh['leaf'=64,'sec'=8] {'sec'}, dimensions={0}, use_global_device_ids=true | all-gather | bytes 73728 | tf_op jit(solution)/shard_map/all_gather | solution.py:31
  65.9 3.6 collective-permute-start.2
  69.6 2.6 collective-permute-done.2
  74.1 6.4 %collective-permute-done.3 = bf16[512,128]{1,0:T(8,128)(2,1)S(1)} collective-permute-done((bf16[512,128]{1,0:T(8,128)(2,1)S(1)}, bf16[512,128]{1,0:T(8,128)(2,1)S(1)}, u32[]{:S(2)}, u32[]{:S(2)}) %collective-permute-start.3) | collective-permute-done | bytes 131104 | tf_op jit(solution)/shard_map/ppermute | solution.py:16
  80.7 12.8 %all_gather.21 = bf16[256,128]{1,0:T(8,128)(2,1)S(1)} all-gather(bf16[32,128]{1,0:T(8,128)(2,1)S(1)} %fusion.9), channel_id=1, replica_groups=mesh['leaf'=64,'sec'=8] {'sec'}, dimensions={0}, use_global_device_ids=true | all-gather | bytes 73728 | tf_op jit(solution)/shard_map/all_gather | solution.py:31
  93.5 3.6 collective-permute-start.4
  97.1 2.6 collective-permute-done.4
  101.9 6.2 %collective-permute-done.5 = bf16[512,128]{1,0:T(8,128)(2,1)S(1)} collective-permute-done((bf16[512,128]{1,0:T(8,128)(2,1)S(1)}, bf16[512,128]{1,0:T(8,128)(2,1)S(1)}, u32[]{:S(2)}, u32[]{:S(2)}) %collective-permute-start.5) | collective-permute-done | bytes 131104 | tf_op jit(solution)/shard_map/ppermute | solution.py:16
  109.1 12.8 %all_gather.22 = bf16[256,128]{1,0:T(8,128)(2,1)S(1)} all-gather(bf16[32,128]{1,0:T(8,128)(2,1)S(1)} %fusion.16), channel_id=1, replica_groups=mesh['leaf'=64,'sec'=8] {'sec'}, dimensions={0}, use_global_device_ids=true | all-gather | bytes 73728 | tf_op jit(solution)/shard_map/all_gather | solution.py:31
  121.9 3.6 collective-permute-start.6
  130.3 6.2 %collective-permute-done.7 = bf16[512,128]{1,0:T(8,128)(2,1)S(1)} collective-permute-done((bf16[512,128]{1,0:T(8,128)(2,1)S(1)}, bf16[512,128]{1,0:T(8,128)(2,1)S(1)}, u32[]{:S(2)}, u32[]{:S(2)}) %collective-permute-start.7) | collective-permute-done | bytes 131104 | tf_op jit(solution)/shard_map/ppermute | solution.py:16
  138.5 6.5 %collective-permute-done.8 = bf16[1024,128]{1,0:T(8,128)(2,1)S(1)} collective-permute-done((bf16[1024,128]{1,0:T(8,128)(2,1)S(1)}, bf16[1024,128]{1,0:T(8,128)(2,1)S(1)}, u32[]{:S(2)}, u32[]{:S(2)}) %collective-permute-start.8) | collective-permute-done | bytes 262176 | tf_op jit(solution)/shard_map/ppermute | solution.py:16
  145.3 12.8 %all_gather.23 = bf16[256,128]{1,0:T(8,128)(2,1)S(1)} all-gather(bf16[32,128]{1,0:T(8,128)(2,1)S(1)} %fusion.10), channel_id=1, replica_groups=mesh['leaf'=64,'sec'=8] {'sec'}, dimensions={0}, use_global_device_ids=true | all-gather | bytes 73728 | tf_op jit(solution)/shard_map/all_gather | solution.py:31
  158.0 3.6 collective-permute-start.9
  161.7 2.6 collective-permute-done.9
  166.5 6.2 %collective-permute-done.10 = bf16[512,128]{1,0:T(8,128)(2,1)S(1)} collective-permute-done((bf16[512,128]{1,0:T(8,128)(2,1)S(1)}, bf16[512,128]{1,0:T(8,128)(2,1)S(1)}, u32[]{:S(2)}, u32[]{:S(2)}) %collective-permute-start.10) | collective-permute-done | bytes 131104 | tf_op jit(solution)/shard_map/ppermute | solution.py:16
  175.0 6.4 %collective-permute-done.11 = bf16[1024,128]{1,0:T(8,128)(2,1)} collective-permute-done((bf16[1024,128]{1,0:T(8,128)(2,1)S(1)}, bf16[1024,128]{1,0:T(8,128)(2,1)}, u32[]{:S(2)}, u32[]{:S(2)}) %collective-permute-start.11) | collective-permute-done | bytes 262176 | tf_op jit(solution)/shard_map/ppermute | solution.py:16
  185.5 11.0 %collective-permute-done.12 = f32[1024,128]{0,1:T(8,128)S(1)} collective-permute-done((f32[1024,128]{0,1:T(8,128)S(1)}, f32[1024,128]{0,1:T(8,128)S(1)}, u32[]{:S(2)}, u32[]{:S(2)}) %collective-permute-start.12) | collective-permute-done | bytes 524320 | tf_op jit(solution)/shard_map/ppermute | solution.py:16
  198.9 8.2 %collective-permute-done.13 = f32[512,128]{0,1:T(8,128)S(1)} collective-permute-done((f32[512,128]{0,1:T(8,128)S(1)}, f32[512,128]{0,1:T(8,128)S(1)}, u32[]{:S(2)}, u32[]{:S(2)}) %collective-permute-start.13) | collective-permute-done | bytes 262176 | tf_op jit(solution)/shard_map/ppermute | solution.py:16
  207.2 3.9 collective-permute-start.14
  211.0 3.0 collective-permute-done.14
  214.9 37.6 %reduce-scatter.19.cloned.1.call-done = f32[32,128]{1,0:T(8,128)} async-done(((f32[256,128]{1,0:T(8,128)}), f32[32,128]{1,0:T(8,128)}) %reduce-scatter.19.cloned.1.call-update) | async-done | bytes 16400
  253.7 3.6 collective-permute-start.15
  257.3 9.5 %collective-permute-done.15 = f32[1024,128]{0,1:T(8,128)S(1)} collective-permute-done((f32[1024,128]{0,1:T(8,128)S(1)}, f32[1024,128]{0,1:T(8,128)S(1)}, u32[]{:S(2)}, u32[]{:S(2)}) %collective-permute-start.15) | collective-permute-done | bytes 524320 | tf_op jit(solution)/shard_map/ppermute | solution.py:16
  266.9 4.1 collective-permute-start.16
  271.0 5.7 %collective-permute-done.16 = f32[512,128]{0,1:T(8,128)S(1)} collective-permute-done((f32[512,128]{0,1:T(8,128)S(1)}, f32[512,128]{0,1:T(8,128)S(1)}, u32[]{:S(2)}, u32[]{:S(2)}) %collective-permute-start.16) | collective-permute-done | bytes 262176 | tf_op jit(solution)/shard_map/ppermute | solution.py:16
  276.7 3.5 collective-permute-start.17
  280.3 3.3 collective-permute-done.17
  284.5 41.8 %reduce-scatter.21.cloned.1.call-done = f32[32,128]{1,0:T(8,128)} async-done(((f32[256,128]{1,0:T(8,128)}), f32[32,128]{1,0:T(8,128)}) %reduce-scatter.21.cloned.1.call-update) | async-done | bytes 16400 | tf_op jit(solution)/shard_map/reduce_scatter | solution.py:50
  327.4 4.0 collective-permute-start.18
  331.4 5.8 %collective-permute-done.18 = f32[512,128]{0,1:T(8,128)S(1)} collective-permute-done((f32[512,128]{0,1:T(8,128)S(1)}, f32[512,128]{0,1:T(8,128)S(1)}, u32[]{:S(2)}, u32[]{:S(2)}) %collective-permute-start.18) | collective-permute-done | bytes 262176 | tf_op jit(solution)/shard_map/ppermute | solution.py:16
  337.2 2.6 collective-permute-start.19
  339.8 4.3 collective-permute-done.19
  344.9 39.3 %reduce-scatter.23.cloned.1.call-done = f32[32,128]{1,0:T(8,128)} async-done(((f32[256,128]{1,0:T(8,128)}), f32[32,128]{1,0:T(8,128)}) %reduce-scatter.23.cloned.1.call-update) | async-done | bytes 16400
  385.4 4.2 collective-permute-start.20
  389.6 5.7 %collective-permute-done.20 = f32[512,128]{0,1:T(8,128)S(1)} collective-permute-done((f32[512,128]{0,1:T(8,128)S(1)}, f32[512,128]{0,1:T(8,128)S(1)}, u32[]{:S(2)}, u32[]{:S(2)}) %collective-permute-start.20) | collective-permute-done | bytes 262176 | tf_op jit(solution)/shard_map/ppermute | solution.py:16
  395.4 2.6 collective-permute-start.21
  397.9 4.3 collective-permute-done.21
  403.1 39.4 %reduce-scatter.25.cloned.1.call-done = f32[32,128]{1,0:T(8,128)} async-done(((f32[256,128]{1,0:T(8,128)}), f32[32,128]{1,0:T(8,128)}) %reduce-scatter.25.cloned.1.call-update) | async-done | bytes 16400 | tf_op jit(solution)/shard_map/reduce_scatter | solution.py:50
  446.0 4.4 collective-permute-done.22
  451.5 37.2 %reduce-scatter.27.cloned.1.call-done = f32[32,128]{1,0:T(8,128)} async-done(((f32[256,128]{1,0:T(8,128)}), f32[32,128]{1,0:T(8,128)}) %reduce-scatter.27.cloned.1.call-update) | async-done | bytes 16400
  492.3 4.3 collective-permute-done.23
  498.1 36.7 %reduce-scatter.29.cloned.1.call-done = f32[32,128]{1,0:T(8,128)} async-done(((f32[256,128]{1,0:T(8,128)}), f32[32,128]{1,0:T(8,128)}) %reduce-scatter.29.cloned.1.call-update) | async-done | bytes 16400
  (110 shorter events, 48.0 us)
Async XLA Ops:
  7.2 2.0 copy-start
  7.2 26.0 %copy-start.3 = (bf16[32,3584]{1,0:T(8,128)(2,1)S(1)}, bf16[32,3584]{1,0:T(8,128)(2,1)}, u32[]{:S(2)}) copy-start(bf16[32,3584]{1,0:T(8,128)(2,1)} %param.16) | copy-start | bytes 688132
  7.2 26.0 %copy-start.8 = (bf16[3,32,128]{2,1,0:T(8,128)(2,1)S(1)}, bf16[3,32,128]{2,1,0:T(8,128)(2,1)}, u32[]{:S(2)}) copy-start(bf16[3,32,128]{2,1,0:T(8,128)(2,1)} %param.17) | copy-start | bytes 73732
  7.2 245.3 %reduce-scatter.19.cloned.1.call-start = ((), (), s32[]{:S(2)}) async-start(), calls=%async_computation.6 | async-start | bytes 147456
  23.3 9.9 %collective-permute-start = (bf16[256,128]{1,0:T(8,128)(2,1)S(1)}, bf16[256,128]{1,0:T(8,128)(2,1)S(1)}, u32[]{:S(2)}, u32[]{:S(2)}) collective-permute-start(bf16[256,128]{1,0:T(8,128)(2,1)S(1)} %all_gather.18), channel_id=1, source_target_pairs={{0,8},{8,0},{16,24},{24,16},{32,40},{40,32},{48,56},{56,48},{64,72... | collective-permute-start | bytes 196616 | tf_op jit(solution)/shard_map/ppermute | solution.py:16
  46.1 6.2 %collective-permute-start.1 = (bf16[256,128]{1,0:T(8,128)(2,1)S(1)}, bf16[256,128]{1,0:T(8,128)(2,1)S(1)}, u32[]{:S(2)}, u32[]{:S(2)}) collective-permute-start(bf16[256,128]{1,0:T(8,128)(2,1)S(1)} %all_gather.19), channel_id=1, source_target_pairs={{0,8},{8,0},{16,24},{24,16},{32,40},{40,32},{48,56},{56,48},{64,72... | collective-permute-start | bytes 196616 | tf_op jit(solution)/shard_map/ppermute | solution.py:16
  65.9 6.2 %collective-permute-start.2 = (bf16[256,128]{1,0:T(8,128)(2,1)S(1)}, bf16[256,128]{1,0:T(8,128)(2,1)S(1)}, u32[]{:S(2)}, u32[]{:S(2)}) collective-permute-start(bf16[256,128]{1,0:T(8,128)(2,1)S(1)} %all_gather.20), channel_id=1, source_target_pairs={{0,8},{8,0},{16,24},{24,16},{32,40},{40,32},{48,56},{56,48},{64,72... | collective-permute-start | bytes 196616 | tf_op jit(solution)/shard_map/ppermute | solution.py:16
  72.2 8.4 %collective-permute-start.3 = (bf16[512,128]{1,0:T(8,128)(2,1)S(1)}, bf16[512,128]{1,0:T(8,128)(2,1)S(1)}, u32[]{:S(2)}, u32[]{:S(2)}) collective-permute-start(bf16[512,128]{1,0:T(8,128)(2,1)S(1)} %maximum_select_fusion.15), channel_id=1, source_target_pairs={{0,16},{16,0},{8,24},{24,8},{32,48},{48,32},{40,56},{56,40},{64,80... | collective-permute-start | bytes 393224 | tf_op jit(solution)/shard_map/ppermute | solution.py:16
  93.5 6.2 %collective-permute-start.4 = (bf16[256,128]{1,0:T(8,128)(2,1)S(1)}, bf16[256,128]{1,0:T(8,128)(2,1)S(1)}, u32[]{:S(2)}, u32[]{:S(2)}) collective-permute-start(bf16[256,128]{1,0:T(8,128)(2,1)S(1)} %all_gather.21), channel_id=1, source_target_pairs={{0,8},{8,0},{16,24},{24,16},{32,40},{40,32},{48,56},{56,48},{64,72... | collective-permute-start | bytes 196616 | tf_op jit(solution)/shard_map/ppermute | solution.py:16
  99.7 8.4 %collective-permute-start.5 = (bf16[512,128]{1,0:T(8,128)(2,1)S(1)}, bf16[512,128]{1,0:T(8,128)(2,1)S(1)}, u32[]{:S(2)}, u32[]{:S(2)}) collective-permute-start(bf16[512,128]{1,0:T(8,128)(2,1)S(1)} %maximum_select_fusion.16), channel_id=1, source_target_pairs={{0,16},{16,0},{8,24},{24,8},{32,48},{48,32},{40,56},{56,40},{64,80... | collective-permute-start | bytes 393224 | tf_op jit(solution)/shard_map/ppermute | solution.py:16
  109.1 72.2 %copy-start.5 = (bf16[3,32,128]{2,1,0:T(8,128)(2,1)S(1)}, bf16[3,32,128]{2,1,0:T(8,128)(2,1)}, u32[]{:S(2)}) copy-start(bf16[3,32,128]{2,1,0:T(8,128)(2,1)} %param.18) | copy-start | bytes 73732
  121.9 6.2 %collective-permute-start.6 = (bf16[256,128]{1,0:T(8,128)(2,1)S(1)}, bf16[256,128]{1,0:T(8,128)(2,1)S(1)}, u32[]{:S(2)}, u32[]{:S(2)}) collective-permute-start(bf16[256,128]{1,0:T(8,128)(2,1)S(1)} %all_gather.22), channel_id=1, source_target_pairs={{0,8},{8,0},{16,24},{24,16},{32,40},{40,32},{48,56},{56,48},{64,72... | collective-permute-start | bytes 196616 | tf_op jit(solution)/shard_map/ppermute | solution.py:16
  128.1 8.4 %collective-permute-start.7 = (bf16[512,128]{1,0:T(8,128)(2,1)S(1)}, bf16[512,128]{1,0:T(8,128)(2,1)S(1)}, u32[]{:S(2)}, u32[]{:S(2)}) collective-permute-start(bf16[512,128]{1,0:T(8,128)(2,1)S(1)} %maximum_select_fusion.17), channel_id=1, source_target_pairs={{0,16},{16,0},{8,24},{24,8},{32,48},{48,32},{40,56},{56,40},{64,80... | collective-permute-start | bytes 393224 | tf_op jit(solution)/shard_map/ppermute | solution.py:16
  136.6 8.5 %collective-permute-start.8 = (bf16[1024,128]{1,0:T(8,128)(2,1)S(1)}, bf16[1024,128]{1,0:T(8,128)(2,1)S(1)}, u32[]{:S(2)}, u32[]{:S(2)}) collective-permute-start(bf16[1024,128]{1,0:T(8,128)(2,1)S(1)} %maximum_select_fusion.9), channel_id=1, source_target_pairs={{0,32},{32,0},{8,40},{40,8},{16,48},{48,16},{24,56},{56,24},{64,96... | collective-permute-start | bytes 786440 | tf_op jit(solution)/shard_map/ppermute | solution.py:16
  158.0 6.2 %collective-permute-start.9 = (bf16[256,128]{1,0:T(8,128)(2,1)S(1)}, bf16[256,128]{1,0:T(8,128)(2,1)S(1)}, u32[]{:S(2)}, u32[]{:S(2)}) collective-permute-start(bf16[256,128]{1,0:T(8,128)(2,1)S(1)} %all_gather.23), channel_id=1, source_target_pairs={{0,8},{8,0},{16,24},{24,16},{32,40},{40,32},{48,56},{56,48},{64,72... | collective-permute-start | bytes 196616 | tf_op jit(solution)/shard_map/ppermute | solution.py:16
  164.3 8.4 %collective-permute-start.10 = (bf16[512,128]{1,0:T(8,128)(2,1)S(1)}, bf16[512,128]{1,0:T(8,128)(2,1)S(1)}, u32[]{:S(2)}, u32[]{:S(2)}) collective-permute-start(bf16[512,128]{1,0:T(8,128)(2,1)S(1)} %maximum_select_fusion.18), channel_id=1, source_target_pairs={{0,16},{16,0},{8,24},{24,8},{32,48},{48,32},{40,56},{56,40},{64,80... | collective-permute-start | bytes 393224 | tf_op jit(solution)/shard_map/ppermute | solution.py:16
  172.7 2.2 copy-start.1
  172.7 8.6 %collective-permute-start.11 = (bf16[1024,128]{1,0:T(8,128)(2,1)S(1)}, bf16[1024,128]{1,0:T(8,128)(2,1)}, u32[]{:S(2)}, u32[]{:S(2)}) collective-permute-start(bf16[1024,128]{1,0:T(8,128)(2,1)S(1)} %maximum_select_fusion.10), channel_id=1, source_target_pairs={{0,32},{32,0},{8,40},{40,8},{16,48},{48,16},{24,56},{56,24},{64,96... | collective-permute-start | bytes 786440 | tf_op jit(solution)/shard_map/ppermute | solution.py:16
  183.3 13.2 %collective-permute-start.12 = (f32[1024,128]{0,1:T(8,128)S(1)}, f32[1024,128]{0,1:T(8,128)S(1)}, u32[]{:S(2)}, u32[]{:S(2)}) collective-permute-start(f32[1024,128]{0,1:T(8,128)S(1)} %slice_select_fusion.1), channel_id=1, source_target_pairs={{0,32},{32,0},{8,40},{40,8},{16,48},{48,16},{24,56},{56,24},{64,96... | collective-permute-start | bytes 1572872 | tf_op jit(solution)/shard_map/ppermute | solution.py:16
  196.5 56.8 %copy-start.4 = (bf16[32,3584]{1,0:T(8,128)(2,1)S(1)}, bf16[32,3584]{1,0:T(8,128)(2,1)}, u32[]{:S(2)}) copy-start(bf16[32,3584]{1,0:T(8,128)(2,1)} %param.16) | copy-start | bytes 688132
  196.6 10.5 %collective-permute-start.13 = (f32[512,128]{0,1:T(8,128)S(1)}, f32[512,128]{0,1:T(8,128)S(1)}, u32[]{:S(2)}, u32[]{:S(2)}) collective-permute-start(f32[512,128]{0,1:T(8,128)S(1)} %slice_select_fusion.5), channel_id=1, source_target_pairs={{0,16},{16,0},{8,24},{24,8},{32,48},{48,32},{40,56},{56,40},{64,80... | collective-permute-start | bytes 786440 | tf_op jit(solution)/shard_map/ppermute | solution.py:16
  207.2 6.9 %collective-permute-start.14 = (f32[256,128]{0,1:T(8,128)S(1)}, f32[256,128]{0,1:T(8,128)S(1)}, u32[]{:S(2)}, u32[]{:S(2)}) collective-permute-start(f32[256,128]{0,1:T(8,128)S(1)} %slice_select_fusion.11), channel_id=1, source_target_pairs={{0,8},{8,0},{16,24},{24,16},{32,40},{40,32},{48,56},{56,48},{64,72... | collective-permute-start | bytes 393224 | tf_op jit(solution)/shard_map/ppermute | solution.py:16
  214.8 111.4 %reduce-scatter.21.cloned.1.call-start = ((), (), s32[]{:S(2)}) async-start(), calls=%async_computation.7 | async-start | bytes 147456 | tf_op jit(solution)/shard_map/reduce_scatter | solution.py:50
  253.7 13.1 %collective-permute-start.15 = (f32[1024,128]{0,1:T(8,128)S(1)}, f32[1024,128]{0,1:T(8,128)S(1)}, u32[]{:S(2)}, u32[]{:S(2)}) collective-permute-start(f32[1024,128]{0,1:T(8,128)S(1)} %slice_select_fusion), channel_id=1, source_target_pairs={{0,32},{32,0},{8,40},{40,8},{16,48},{48,16},{24,56},{56,24},{64,96... | collective-permute-start | bytes 1572872 | tf_op jit(solution)/shard_map/ppermute | solution.py:16
  266.9 9.8 %collective-permute-start.16 = (f32[512,128]{0,1:T(8,128)S(1)}, f32[512,128]{0,1:T(8,128)S(1)}, u32[]{:S(2)}, u32[]{:S(2)}) collective-permute-start(f32[512,128]{0,1:T(8,128)S(1)} %slice_select_fusion.4), channel_id=1, source_target_pairs={{0,16},{16,0},{8,24},{24,8},{32,48},{48,32},{40,56},{56,40},{64,80... | collective-permute-start | bytes 786440 | tf_op jit(solution)/shard_map/ppermute | solution.py:16
  276.7 6.9 %collective-permute-start.17 = (f32[256,128]{0,1:T(8,128)S(1)}, f32[256,128]{0,1:T(8,128)S(1)}, u32[]{:S(2)}, u32[]{:S(2)}) collective-permute-start(f32[256,128]{0,1:T(8,128)S(1)} %slice_select_fusion.10), channel_id=1, source_target_pairs={{0,8},{8,0},{16,24},{24,16},{32,40},{40,32},{48,56},{56,48},{64,72... | collective-permute-start | bytes 393224 | tf_op jit(solution)/shard_map/ppermute | solution.py:16
  284.4 99.9 %reduce-scatter.23.cloned.1.call-start = ((), (), s32[]{:S(2)}) async-start(), calls=%async_computation.8 | async-start | bytes 147456
  327.4 9.8 %collective-permute-start.18 = (f32[512,128]{0,1:T(8,128)S(1)}, f32[512,128]{0,1:T(8,128)S(1)}, u32[]{:S(2)}, u32[]{:S(2)}) collective-permute-start(f32[512,128]{0,1:T(8,128)S(1)} %slice_select_fusion.3), channel_id=1, source_target_pairs={{0,16},{16,0},{8,24},{24,8},{32,48},{48,32},{40,56},{56,40},{64,80... | collective-permute-start | bytes 786440 | tf_op jit(solution)/shard_map/ppermute | solution.py:16
  337.2 6.9 %collective-permute-start.19 = (f32[256,128]{0,1:T(8,128)S(1)}, f32[256,128]{0,1:T(8,128)S(1)}, u32[]{:S(2)}, u32[]{:S(2)}) collective-permute-start(f32[256,128]{0,1:T(8,128)S(1)} %slice_select_fusion.9), channel_id=1, source_target_pairs={{0,8},{8,0},{16,24},{24,16},{32,40},{40,32},{48,56},{56,48},{64,72... | collective-permute-start | bytes 393224 | tf_op jit(solution)/shard_map/ppermute | solution.py:16
  344.9 97.6 %reduce-scatter.25.cloned.1.call-start = ((), (), s32[]{:S(2)}) async-start(), calls=%async_computation.9 | async-start | bytes 147456 | tf_op jit(solution)/shard_map/reduce_scatter | solution.py:50
  385.3 65.9 %copy-start.6 = (bf16[3,32]{1,0:T(4,128)(2,1)S(1)}, bf16[3,32]{1,0:T(4,128)(2,1)}, u32[]{:S(2)}) copy-start(bf16[3,32]{1,0:T(4,128)(2,1)} %param.19) | copy-start | bytes 580
  385.3 65.9 %copy-start.2 = (bf16[1024,128]{1,0:T(8,128)(2,1)S(1)}, bf16[1024,128]{1,0:T(8,128)(2,1)}, u32[]{:S(2)}) copy-start(bf16[1024,128]{1,0:T(8,128)(2,1)} %param.13) | copy-start | bytes 786436
  385.4 66.1 %copy-start.7 = (bf16[1024]{0:T(1024)(128)(2,1)S(1)}, bf16[1024]{0:T(1024)(128)(2,1)}, u32[]{:S(2)}) copy-start(bf16[1024]{0:T(1024)(128)(2,1)} %param.14) | copy-start | bytes 6148
  385.4 9.9 %collective-permute-start.20 = (f32[512,128]{0,1:T(8,128)S(1)}, f32[512,128]{0,1:T(8,128)S(1)}, u32[]{:S(2)}, u32[]{:S(2)}) collective-permute-start(f32[512,128]{0,1:T(8,128)S(1)} %slice_select_fusion.2), channel_id=1, source_target_pairs={{0,16},{16,0},{8,24},{24,8},{32,48},{48,32},{40,56},{56,40},{64,80... | collective-permute-start | bytes 786440 | tf_op jit(solution)/shard_map/ppermute | solution.py:16
  395.4 6.9 %collective-permute-start.21 = (f32[256,128]{0,1:T(8,128)S(1)}, f32[256,128]{0,1:T(8,128)S(1)}, u32[]{:S(2)}, u32[]{:S(2)}) collective-permute-start(f32[256,128]{0,1:T(8,128)S(1)} %slice_select_fusion.8), channel_id=1, source_target_pairs={{0,8},{8,0},{16,24},{24,16},{32,40},{40,32},{48,56},{56,48},{64,72... | collective-permute-start | bytes 393224 | tf_op jit(solution)/shard_map/ppermute | solution.py:16
  403.0 85.7 %reduce-scatter.27.cloned.1.call-start = ((), (), s32[]{:S(2)}) async-start(), calls=%async_computation.10 | async-start | bytes 147456
  443.5 6.9 %collective-permute-start.22 = (f32[256,128]{0,1:T(8,128)S(1)}, f32[256,128]{0,1:T(8,128)S(1)}, u32[]{:S(2)}, u32[]{:S(2)}) collective-permute-start(f32[256,128]{0,1:T(8,128)S(1)} %slice_select_fusion.7), channel_id=1, source_target_pairs={{0,8},{8,0},{16,24},{24,16},{32,40},{40,32},{48,56},{56,48},{64,72... | collective-permute-start | bytes 393224 | tf_op jit(solution)/shard_map/ppermute | solution.py:16
  451.2 83.6 %reduce-scatter.29.cloned.1.call-start = ((), (), s32[]{:S(2)}) async-start(), calls=%async_computation.11 | async-start | bytes 147456
  489.7 6.9 %collective-permute-start.23 = (f32[256,128]{0,1:T(8,128)S(1)}, f32[256,128]{0,1:T(8,128)S(1)}, u32[]{:S(2)}, u32[]{:S(2)}) collective-permute-start(f32[256,128]{0,1:T(8,128)S(1)} %slice_select_fusion.6), channel_id=1, source_target_pairs={{0,8},{8,0},{16,24},{24,16},{32,40},{40,32},{48,56},{56,48},{64,72... | collective-permute-start | bytes 393224 | tf_op jit(solution)/shard_map/ppermute | solution.py:16
Sparse Core Ops, SparseCore 0:
  215.0 37.4 reduce-scatter.18
  284.5 41.6 reduce-scatter.20
  345.0 39.2 reduce-scatter.22
  403.1 39.3 reduce-scatter.24
  451.3 37.3 reduce-scatter.26
  497.5 37.2 reduce-scatter.28
where the time goes:
time: 545 us; the launch traced here: 544 us
  waiting for transfers between devices  355 us (65%)
  blocking collectives  76.8 us (14%)
  starting transfers between devices  76.1 us (14%)
  between operations  15.5 us (3%)
  local copies, waits for them, and re-layouts  10.3 us (2%)
  matrix products  8.35 us (2%)
    unnamed x10, waiting for transfers between devices  151 us
    ppermute x24, waiting for transfers between devices, from_partner(): return lax.ppermute(block, axis, route)  123 us
    reduce_scatter x2, waiting for transfers between devices, group_reduce(): return lax.psum_scatter(reduced, 'sec', scatter_dimension=0, tiled=True)  81.2 us
    all_gather x6, blocking collectives, group_gather(): block = lax.all_gather(piece, 'sec', axis=0, tiled=True)  76.8 us
    ppermute x24, starting transfers between devices, from_partner(): return lax.ppermute(block, axis, route)  75.9 us
  transfers between devices with their start and end apart: 30, of which 30 were waited for; matrix products, arithmetic and copies ran while one was open for 0% of the time, Pallas kernels for 0%

commit v1 on v0

--- a/solution.py
+++ b/solution.py
@@ -28,7 +28,9 @@
 
 
 def group_gather(piece, height):
-    block = lax.all_gather(piece, "sec", axis=0, tiled=True)
+    block = jnp.concatenate(
+        lax.all_to_all(jnp.stack([piece] * lax.axis_size("sec")), "sec", 0, 0), axis=0
+    )
     return pair_gather(block, height)
 
 

time: 545 us -> 516 us (0.947)
  the two profiles are of different devices: /device:TPU:8 before, /device:TPU:16 now
where the time goes in v1:
time: 516 us; the launch traced here: 514 us
  waiting for transfers between devices  343 us (66%)
  starting transfers between devices  85.7 us (17%)
  blocking collectives  49.7 us (10%)
  between operations  15.6 us (3%)
  local copies, waits for them, and re-layouts  10.4 us (2%)
  matrix products  8.36 us (2%)
    unnamed x10, waiting for transfers between devices  154 us
    ppermute x24, waiting for transfers between devices, from_partner(): return lax.ppermute(block, axis, route)  108 us
    ppermute x24, starting transfers between devices, from_partner(): return lax.ppermute(block, axis, route)  85.4 us
    reduce_scatter x2, waiting for transfers between devices, group_reduce(): return lax.psum_scatter(reduced, 'sec', scatter_dimension=0, tiled=True)  81 us
    all_to_all x6, blocking collectives, group_gather(): lax.all_to_all(jnp.stack([piece] * lax.axis_size('sec')), 'sec', 0, 0)  49.7 us
  transfers between devices with their start and end apart: 30, of which 30 were waited for; matrix products, arithmetic and copies ran while one was open for 0% of the time, Pallas kernels for 0%

profile of v1, /device:TPU:16, one launch (start us, length us, event | category | flops | bytes accessed | tf_op | source)
XLA Modules:
  0.0 514.4 jit_solution(8659630714993320025)
XLA Ops:
  10.2 9.7 %all_to_all.30 = bf16[8,32,128]{2,1,0:T(8,128)(2,1)S(1)} all-to-all(bf16[8,32,128]{2,1,0:T(8,128)(2,1)S(1)} %stack.20), channel_id=1, replica_groups=mesh['leaf'=64,'sec'=8] {'sec'}, dimensions={0} | all-to-all | bytes 131072 | tf_op jit(solution)/shard_map/all_to_all | solution.py:32
  19.9 3.2 collective-permute-start
  26.2 8.0 %all_to_all.31 = bf16[8,32,128]{2,1,0:T(8,128)(2,1)S(1)} all-to-all(bf16[8,32,128]{2,1,0:T(8,128)(2,1)S(1)} %stack.21), channel_id=1, replica_groups=mesh['leaf'=64,'sec'=8] {'sec'}, dimensions={0} | all-to-all | bytes 131072 | tf_op jit(solution)/shard_map/all_to_all | solution.py:32
  34.2 3.2 collective-permute-start.1
  37.4 3.0 collective-permute-done.1
  41.3 8.0 %all_to_all.32 = bf16[8,32,128]{2,1,0:T(8,128)(2,1)S(1)} all-to-all(bf16[8,32,128]{2,1,0:T(8,128)(2,1)S(1)} %stack.22), channel_id=1, replica_groups=mesh['leaf'=64,'sec'=8] {'sec'}, dimensions={0} | all-to-all | bytes 131072 | tf_op jit(solution)/shard_map/all_to_all | solution.py:32
  49.3 3.2 collective-permute-start.2
  55.5 5.9 %collective-permute-start.3 = (bf16[512,128]{1,0:T(8,128)(2,1)S(1)}, bf16[512,128]{1,0:T(8,128)(2,1)S(1)}, u32[]{:S(2)}, u32[]{:S(2)}) collective-permute-start(bf16[512,128]{1,0:T(8,128)(2,1)S(1)} %maximum_select_fusion.15), channel_id=1, source_target_pairs={{0,16},{16,0},{8,24},{24,8},{32,48},{48,32},{40,56},{56,40},{64,80... | collective-permute-start | bytes 393224 | tf_op jit(solution)/shard_map/ppermute | solution.py:16
  64.5 8.0 %all_to_all.33 = bf16[8,32,128]{2,1,0:T(8,128)(2,1)S(1)} all-to-all(bf16[8,32,128]{2,1,0:T(8,128)(2,1)S(1)} %stack.23), channel_id=1, replica_groups=mesh['leaf'=64,'sec'=8] {'sec'}, dimensions={0} | all-to-all | bytes 131072 | tf_op jit(solution)/shard_map/all_to_all | solution.py:32
  75.2 3.4 collective-permute-done.4
  78.7 5.4 %collective-permute-start.5 = (bf16[512,128]{1,0:T(8,128)(2,1)S(1)}, bf16[512,128]{1,0:T(8,128)(2,1)S(1)}, u32[]{:S(2)}, u32[]{:S(2)}) collective-permute-start(bf16[512,128]{1,0:T(8,128)(2,1)S(1)} %maximum_select_fusion.16), channel_id=1, source_target_pairs={{0,16},{16,0},{8,24},{24,8},{32,48},{48,32},{40,56},{56,40},{64,80... | collective-permute-start | bytes 393224 | tf_op jit(solution)/shard_map/ppermute | solution.py:16
  88.1 8.0 %all_to_all.34 = bf16[8,32,128]{2,1,0:T(8,128)(2,1)S(1)} all-to-all(bf16[8,32,128]{2,1,0:T(8,128)(2,1)S(1)} %stack.24), channel_id=1, replica_groups=mesh['leaf'=64,'sec'=8] {'sec'}, dimensions={0} | all-to-all | bytes 131072 | tf_op jit(solution)/shard_map/all_to_all | solution.py:32
  98.8 3.4 collective-permute-done.6
  102.3 5.4 %collective-permute-start.7 = (bf16[512,128]{1,0:T(8,128)(2,1)S(1)}, bf16[512,128]{1,0:T(8,128)(2,1)S(1)}, u32[]{:S(2)}, u32[]{:S(2)}) collective-permute-start(bf16[512,128]{1,0:T(8,128)(2,1)S(1)} %maximum_select_fusion.17), channel_id=1, source_target_pairs={{0,16},{16,0},{8,24},{24,8},{32,48},{48,32},{40,56},{56,40},{64,80... | collective-permute-start | bytes 393224 | tf_op jit(solution)/shard_map/ppermute | solution.py:16
  110.8 3.4 collective-permute-start.8
  114.1 4.9 collective-permute-done.8
  119.3 8.0 %all_to_all.35 = bf16[8,32,128]{2,1,0:T(8,128)(2,1)S(1)} all-to-all(bf16[8,32,128]{2,1,0:T(8,128)(2,1)S(1)} %stack.25), channel_id=1, replica_groups=mesh['leaf'=64,'sec'=8] {'sec'}, dimensions={0} | all-to-all | bytes 131072 | tf_op jit(solution)/shard_map/all_to_all | solution.py:32
  130.0 3.4 collective-permute-done.9
  133.5 5.4 %collective-permute-start.10 = (bf16[512,128]{1,0:T(8,128)(2,1)S(1)}, bf16[512,128]{1,0:T(8,128)(2,1)S(1)}, u32[]{:S(2)}, u32[]{:S(2)}) collective-permute-start(bf16[512,128]{1,0:T(8,128)(2,1)S(1)} %maximum_select_fusion.18), channel_id=1, source_target_pairs={{0,16},{16,0},{8,24},{24,8},{32,48},{48,32},{40,56},{56,40},{64,80... | collective-permute-start | bytes 393224 | tf_op jit(solution)/shard_map/ppermute | solution.py:16
  142.0 3.4 collective-permute-start.11
  145.3 5.0 collective-permute-done.11
  152.3 3.4 collective-permute-start.12
  155.6 8.9 %collective-permute-done.12 = f32[1024,128]{0,1:T(8,128)S(1)} collective-permute-done((f32[1024,128]{0,1:T(8,128)S(1)}, f32[1024,128]{0,1:T(8,128)S(1)}, u32[]{:S(2)}, u32[]{:S(2)}) %collective-permute-start.12) | collective-permute-done | bytes 524320 | tf_op jit(solution)/shard_map/ppermute | solution.py:16
  164.7 5.3 %collective-permute-start.13 = (f32[512,128]{0,1:T(8,128)S(1)}, f32[512,128]{0,1:T(8,128)S(1)}, u32[]{:S(2)}, u32[]{:S(2)}) collective-permute-start(f32[512,128]{0,1:T(8,128)S(1)} %slice_select_fusion.5), channel_id=1, source_target_pairs={{0,16},{16,0},{8,24},{24,8},{32,48},{48,32},{40,56},{56,40},{64,80... | collective-permute-start | bytes 786440 | tf_op jit(solution)/shard_map/ppermute | solution.py:16
  170.0 5.3 %collective-permute-done.13 = f32[512,128]{0,1:T(8,128)S(1)} collective-permute-done((f32[512,128]{0,1:T(8,128)S(1)}, f32[512,128]{0,1:T(8,128)S(1)}, u32[]{:S(2)}, u32[]{:S(2)}) %collective-permute-start.13) | collective-permute-done | bytes 262176 | tf_op jit(solution)/shard_map/ppermute | solution.py:16
  178.2 4.1 collective-permute-done.14
  183.1 40.4 %reduce-scatter.19.cloned.1.call-done = f32[32,128]{1,0:T(8,128)} async-done(((f32[256,128]{1,0:T(8,128)}), f32[32,128]{1,0:T(8,128)}) %reduce-scatter.19.cloned.1.call-update) | async-done | bytes 16400
  224.6 3.4 collective-permute-start.15
  228.1 9.6 %collective-permute-done.15 = f32[1024,128]{0,1:T(8,128)S(1)} collective-permute-done((f32[1024,128]{0,1:T(8,128)S(1)}, f32[1024,128]{0,1:T(8,128)S(1)}, u32[]{:S(2)}, u32[]{:S(2)}) %collective-permute-start.15) | collective-permute-done | bytes 524320 | tf_op jit(solution)/shard_map/ppermute | solution.py:16
  237.8 3.3 collective-permute-start.16
  241.1 6.4 %collective-permute-done.16 = f32[512,128]{0,1:T(8,128)S(1)} collective-permute-done((f32[512,128]{0,1:T(8,128)S(1)}, f32[512,128]{0,1:T(8,128)S(1)}, u32[]{:S(2)}, u32[]{:S(2)}) %collective-permute-start.16) | collective-permute-done | bytes 262176 | tf_op jit(solution)/shard_map/ppermute | solution.py:16
  247.6 3.1 collective-permute-start.17
  250.7 3.8 collective-permute-done.17
  255.4 41.6 %reduce-scatter.21.cloned.1.call-done = f32[32,128]{1,0:T(8,128)} async-done(((f32[256,128]{1,0:T(8,128)}), f32[32,128]{1,0:T(8,128)}) %reduce-scatter.21.cloned.1.call-update) | async-done | bytes 16400 | tf_op jit(solution)/shard_map/reduce_scatter | solution.py:52
  300.5 7.3 %collective-permute-done.18 = f32[512,128]{0,1:T(8,128)S(1)} collective-permute-done((f32[512,128]{0,1:T(8,128)S(1)}, f32[512,128]{0,1:T(8,128)S(1)}, u32[]{:S(2)}, u32[]{:S(2)}) %collective-permute-start.18) | collective-permute-done | bytes 262176 | tf_op jit(solution)/shard_map/ppermute | solution.py:16
  307.9 3.1 collective-permute-start.19
  311.0 3.8 collective-permute-done.19
  315.7 39.2 %reduce-scatter.23.cloned.1.call-done = f32[32,128]{1,0:T(8,128)} async-done(((f32[256,128]{1,0:T(8,128)}), f32[32,128]{1,0:T(8,128)}) %reduce-scatter.23.cloned.1.call-update) | async-done | bytes 16400
  358.6 7.3 %collective-permute-done.20 = f32[512,128]{0,1:T(8,128)S(1)} collective-permute-done((f32[512,128]{0,1:T(8,128)S(1)}, f32[512,128]{0,1:T(8,128)S(1)}, u32[]{:S(2)}, u32[]{:S(2)}) %collective-permute-start.20) | collective-permute-done | bytes 262176 | tf_op jit(solution)/shard_map/ppermute | solution.py:16
  366.0 3.1 collective-permute-start.21
  369.1 3.7 collective-permute-done.21
  373.7 39.4 %reduce-scatter.25.cloned.1.call-done = f32[32,128]{1,0:T(8,128)} async-done(((f32[256,128]{1,0:T(8,128)}), f32[32,128]{1,0:T(8,128)}) %reduce-scatter.25.cloned.1.call-update) | async-done | bytes 16400 | tf_op jit(solution)/shard_map/reduce_scatter | solution.py:52
  414.2 3.1 collective-permute-start.22
  417.3 3.7 collective-permute-done.22
  422.2 37.0 %reduce-scatter.27.cloned.1.call-done = f32[32,128]{1,0:T(8,128)} async-done(((f32[256,128]{1,0:T(8,128)}), f32[32,128]{1,0:T(8,128)}) %reduce-scatter.27.cloned.1.call-update) | async-done | bytes 16400
  460.2 3.2 collective-permute-start.23
  463.5 3.6 collective-permute-done.23
  468.6 36.9 %reduce-scatter.29.cloned.1.call-done = f32[32,128]{1,0:T(8,128)} async-done(((f32[256,128]{1,0:T(8,128)}), f32[32,128]{1,0:T(8,128)}) %reduce-scatter.29.cloned.1.call-update) | async-done | bytes 16400
  (116 shorter events, 54.6 us)
Async XLA Ops:
  7.2 2.0 copy-start
  7.2 18.9 %copy-start.3 = (bf16[32,3584]{1,0:T(8,128)(2,1)S(1)}, bf16[32,3584]{1,0:T(8,128)(2,1)}, u32[]{:S(2)}) copy-start(bf16[32,3584]{1,0:T(8,128)(2,1)} %param.16) | copy-start | bytes 688132
  7.2 18.9 %copy-start.8 = (bf16[3,32,128]{2,1,0:T(8,128)(2,1)S(1)}, bf16[3,32,128]{2,1,0:T(8,128)(2,1)}, u32[]{:S(2)}) copy-start(bf16[3,32,128]{2,1,0:T(8,128)(2,1)} %param.17) | copy-start | bytes 73732
  7.2 216.2 %reduce-scatter.19.cloned.1.call-start = ((), (), s32[]{:S(2)}) async-start(), calls=%async_computation.12 | async-start | bytes 147456
  19.9 6.1 %collective-permute-start = (bf16[256,128]{1,0:T(8,128)(2,1)S(1)}, bf16[256,128]{1,0:T(8,128)(2,1)S(1)}, u32[]{:S(2)}, u32[]{:S(2)}) collective-permute-start(bf16[256,128]{1,0:T(8,128)(2,1)S(1)} %bitcast.114), channel_id=1, source_target_pairs={{0,8},{8,0},{16,24},{24,16},{32,40},{40,32},{48,56},{56,48},{64,72... | collective-permute-start | bytes 196616 | tf_op jit(solution)/shard_map/ppermute | solution.py:16
  34.2 6.1 %collective-permute-start.1 = (bf16[256,128]{1,0:T(8,128)(2,1)S(1)}, bf16[256,128]{1,0:T(8,128)(2,1)S(1)}, u32[]{:S(2)}, u32[]{:S(2)}) collective-permute-start(bf16[256,128]{1,0:T(8,128)(2,1)S(1)} %bitcast.116), channel_id=1, source_target_pairs={{0,8},{8,0},{16,24},{24,16},{32,40},{40,32},{48,56},{56,48},{64,72... | collective-permute-start | bytes 196616 | tf_op jit(solution)/shard_map/ppermute | solution.py:16
  49.3 6.1 %collective-permute-start.2 = (bf16[256,128]{1,0:T(8,128)(2,1)S(1)}, bf16[256,128]{1,0:T(8,128)(2,1)S(1)}, u32[]{:S(2)}, u32[]{:S(2)}) collective-permute-start(bf16[256,128]{1,0:T(8,128)(2,1)S(1)} %bitcast.106), channel_id=1, source_target_pairs={{0,8},{8,0},{16,24},{24,16},{32,40},{40,32},{48,56},{56,48},{64,72... | collective-permute-start | bytes 196616 | tf_op jit(solution)/shard_map/ppermute | solution.py:16
  55.5 8.8 %collective-permute-start.3 = (bf16[512,128]{1,0:T(8,128)(2,1)S(1)}, bf16[512,128]{1,0:T(8,128)(2,1)S(1)}, u32[]{:S(2)}, u32[]{:S(2)}) collective-permute-start(bf16[512,128]{1,0:T(8,128)(2,1)S(1)} %maximum_select_fusion.15), channel_id=1, source_target_pairs={{0,16},{16,0},{8,24},{24,8},{32,48},{48,32},{40,56},{56,40},{64,80... | collective-permute-start | bytes 393224 | tf_op jit(solution)/shard_map/ppermute | solution.py:16
  72.5 6.1 %collective-permute-start.4 = (bf16[256,128]{1,0:T(8,128)(2,1)S(1)}, bf16[256,128]{1,0:T(8,128)(2,1)S(1)}, u32[]{:S(2)}, u32[]{:S(2)}) collective-permute-start(bf16[256,128]{1,0:T(8,128)(2,1)S(1)} %bitcast.108), channel_id=1, source_target_pairs={{0,8},{8,0},{16,24},{24,16},{32,40},{40,32},{48,56},{56,48},{64,72... | collective-permute-start | bytes 196616 | tf_op jit(solution)/shard_map/ppermute | solution.py:16
  78.7 8.4 %collective-permute-start.5 = (bf16[512,128]{1,0:T(8,128)(2,1)S(1)}, bf16[512,128]{1,0:T(8,128)(2,1)S(1)}, u32[]{:S(2)}, u32[]{:S(2)}) collective-permute-start(bf16[512,128]{1,0:T(8,128)(2,1)S(1)} %maximum_select_fusion.16), channel_id=1, source_target_pairs={{0,16},{16,0},{8,24},{24,8},{32,48},{48,32},{40,56},{56,40},{64,80... | collective-permute-start | bytes 393224 | tf_op jit(solution)/shard_map/ppermute | solution.py:16
  88.1 62.2 %copy-start.5 = (bf16[3,32,128]{2,1,0:T(8,128)(2,1)S(1)}, bf16[3,32,128]{2,1,0:T(8,128)(2,1)}, u32[]{:S(2)}) copy-start(bf16[3,32,128]{2,1,0:T(8,128)(2,1)} %param.18) | copy-start | bytes 73732
  96.1 6.1 %collective-permute-start.6 = (bf16[256,128]{1,0:T(8,128)(2,1)S(1)}, bf16[256,128]{1,0:T(8,128)(2,1)S(1)}, u32[]{:S(2)}, u32[]{:S(2)}) collective-permute-start(bf16[256,128]{1,0:T(8,128)(2,1)S(1)} %bitcast.110), channel_id=1, source_target_pairs={{0,8},{8,0},{16,24},{24,16},{32,40},{40,32},{48,56},{56,48},{64,72... | collective-permute-start | bytes 196616 | tf_op jit(solution)/shard_map/ppermute | solution.py:16
  102.3 8.4 %collective-permute-start.7 = (bf16[512,128]{1,0:T(8,128)(2,1)S(1)}, bf16[512,128]{1,0:T(8,128)(2,1)S(1)}, u32[]{:S(2)}, u32[]{:S(2)}) collective-permute-start(bf16[512,128]{1,0:T(8,128)(2,1)S(1)} %maximum_select_fusion.17), channel_id=1, source_target_pairs={{0,16},{16,0},{8,24},{24,8},{32,48},{48,32},{40,56},{56,40},{64,80... | collective-permute-start | bytes 393224 | tf_op jit(solution)/shard_map/ppermute | solution.py:16
  110.8 8.3 %collective-permute-start.8 = (bf16[1024,128]{1,0:T(8,128)(2,1)S(1)}, bf16[1024,128]{1,0:T(8,128)(2,1)S(1)}, u32[]{:S(2)}, u32[]{:S(2)}) collective-permute-start(bf16[1024,128]{1,0:T(8,128)(2,1)S(1)} %maximum_select_fusion.9), channel_id=1, source_target_pairs={{0,32},{32,0},{8,40},{40,8},{16,48},{48,16},{24,56},{56,24},{64,96... | collective-permute-start | bytes 786440 | tf_op jit(solution)/shard_map/ppermute | solution.py:16
  127.3 6.1 %collective-permute-start.9 = (bf16[256,128]{1,0:T(8,128)(2,1)S(1)}, bf16[256,128]{1,0:T(8,128)(2,1)S(1)}, u32[]{:S(2)}, u32[]{:S(2)}) collective-permute-start(bf16[256,128]{1,0:T(8,128)(2,1)S(1)} %bitcast.112), channel_id=1, source_target_pairs={{0,8},{8,0},{16,24},{24,16},{32,40},{40,32},{48,56},{56,48},{64,72... | collective-permute-start | bytes 196616 | tf_op jit(solution)/shard_map/ppermute | solution.py:16
  133.5 8.4 %collective-permute-start.10 = (bf16[512,128]{1,0:T(8,128)(2,1)S(1)}, bf16[512,128]{1,0:T(8,128)(2,1)S(1)}, u32[]{:S(2)}, u32[]{:S(2)}) collective-permute-start(bf16[512,128]{1,0:T(8,128)(2,1)S(1)} %maximum_select_fusion.18), channel_id=1, source_target_pairs={{0,16},{16,0},{8,24},{24,8},{32,48},{48,32},{40,56},{56,40},{64,80... | collective-permute-start | bytes 393224 | tf_op jit(solution)/shard_map/ppermute | solution.py:16
  142.0 3.4 copy-start.1
  142.0 8.4 %collective-permute-start.11 = (bf16[1024,128]{1,0:T(8,128)(2,1)S(1)}, bf16[1024,128]{1,0:T(8,128)(2,1)}, u32[]{:S(2)}, u32[]{:S(2)}) collective-permute-start(bf16[1024,128]{1,0:T(8,128)(2,1)S(1)} %maximum_select_fusion.10), channel_id=1, source_target_pairs={{0,32},{32,0},{8,40},{40,8},{16,48},{48,16},{24,56},{56,24},{64,96... | collective-permute-start | bytes 786440 | tf_op jit(solution)/shard_map/ppermute | solution.py:16
  152.3 12.3 %collective-permute-start.12 = (f32[1024,128]{0,1:T(8,128)S(1)}, f32[1024,128]{0,1:T(8,128)S(1)}, u32[]{:S(2)}, u32[]{:S(2)}) collective-permute-start(f32[1024,128]{0,1:T(8,128)S(1)} %slice_select_fusion.1), channel_id=1, source_target_pairs={{0,32},{32,0},{8,40},{40,8},{16,48},{48,16},{24,56},{56,24},{64,96... | collective-permute-start | bytes 1572872 | tf_op jit(solution)/shard_map/ppermute | solution.py:16
  164.6 59.6 %copy-start.4 = (bf16[32,3584]{1,0:T(8,128)(2,1)S(1)}, bf16[32,3584]{1,0:T(8,128)(2,1)}, u32[]{:S(2)}) copy-start(bf16[32,3584]{1,0:T(8,128)(2,1)} %param.16) | copy-start | bytes 688132
  164.7 10.6 %collective-permute-start.13 = (f32[512,128]{0,1:T(8,128)S(1)}, f32[512,128]{0,1:T(8,128)S(1)}, u32[]{:S(2)}, u32[]{:S(2)}) collective-permute-start(f32[512,128]{0,1:T(8,128)S(1)} %slice_select_fusion.5), channel_id=1, source_target_pairs={{0,16},{16,0},{8,24},{24,8},{32,48},{48,32},{40,56},{56,40},{64,80... | collective-permute-start | bytes 786440 | tf_op jit(solution)/shard_map/ppermute | solution.py:16
  175.4 6.9 %collective-permute-start.14 = (f32[256,128]{0,1:T(8,128)S(1)}, f32[256,128]{0,1:T(8,128)S(1)}, u32[]{:S(2)}, u32[]{:S(2)}) collective-permute-start(f32[256,128]{0,1:T(8,128)S(1)} %slice_select_fusion.11), channel_id=1, source_target_pairs={{0,8},{8,0},{16,24},{24,16},{32,40},{40,32},{48,56},{56,48},{64,72... | collective-permute-start | bytes 393224 | tf_op jit(solution)/shard_map/ppermute | solution.py:16
  183.0 113.9 %reduce-scatter.21.cloned.1.call-start = ((), (), s32[]{:S(2)}) async-start(), calls=%async_computation.13 | async-start | bytes 147456 | tf_op jit(solution)/shard_map/reduce_scatter | solution.py:52
  224.6 13.0 %collective-permute-start.15 = (f32[1024,128]{0,1:T(8,128)S(1)}, f32[1024,128]{0,1:T(8,128)S(1)}, u32[]{:S(2)}, u32[]{:S(2)}) collective-permute-start(f32[1024,128]{0,1:T(8,128)S(1)} %slice_select_fusion), channel_id=1, source_target_pairs={{0,32},{32,0},{8,40},{40,8},{16,48},{48,16},{24,56},{56,24},{64,96... | collective-permute-start | bytes 1572872 | tf_op jit(solution)/shard_map/ppermute | solution.py:16
  237.8 9.8 %collective-permute-start.16 = (f32[512,128]{0,1:T(8,128)S(1)}, f32[512,128]{0,1:T(8,128)S(1)}, u32[]{:S(2)}, u32[]{:S(2)}) collective-permute-start(f32[512,128]{0,1:T(8,128)S(1)} %slice_select_fusion.4), channel_id=1, source_target_pairs={{0,16},{16,0},{8,24},{24,8},{32,48},{48,32},{40,56},{56,40},{64,80... | collective-permute-start | bytes 786440 | tf_op jit(solution)/shard_map/ppermute | solution.py:16
  247.6 6.9 %collective-permute-start.17 = (f32[256,128]{0,1:T(8,128)S(1)}, f32[256,128]{0,1:T(8,128)S(1)}, u32[]{:S(2)}, u32[]{:S(2)}) collective-permute-start(f32[256,128]{0,1:T(8,128)S(1)} %slice_select_fusion.10), channel_id=1, source_target_pairs={{0,8},{8,0},{16,24},{24,16},{32,40},{40,32},{48,56},{56,48},{64,72... | collective-permute-start | bytes 393224 | tf_op jit(solution)/shard_map/ppermute | solution.py:16
  255.3 99.6 %reduce-scatter.23.cloned.1.call-start = ((), (), s32[]{:S(2)}) async-start(), calls=%async_computation.14 | async-start | bytes 147456
  298.1 9.8 %collective-permute-start.18 = (f32[512,128]{0,1:T(8,128)S(1)}, f32[512,128]{0,1:T(8,128)S(1)}, u32[]{:S(2)}, u32[]{:S(2)}) collective-permute-start(f32[512,128]{0,1:T(8,128)S(1)} %slice_select_fusion.3), channel_id=1, source_target_pairs={{0,16},{16,0},{8,24},{24,8},{32,48},{48,32},{40,56},{56,40},{64,80... | collective-permute-start | bytes 786440 | tf_op jit(solution)/shard_map/ppermute | solution.py:16
  307.9 6.9 %collective-permute-start.19 = (f32[256,128]{0,1:T(8,128)S(1)}, f32[256,128]{0,1:T(8,128)S(1)}, u32[]{:S(2)}, u32[]{:S(2)}) collective-permute-start(f32[256,128]{0,1:T(8,128)S(1)} %slice_select_fusion.9), channel_id=1, source_target_pairs={{0,8},{8,0},{16,24},{24,16},{32,40},{40,32},{48,56},{56,48},{64,72... | collective-permute-start | bytes 393224 | tf_op jit(solution)/shard_map/ppermute | solution.py:16
  315.6 97.5 %reduce-scatter.25.cloned.1.call-start = ((), (), s32[]{:S(2)}) async-start(), calls=%async_computation.15 | async-start | bytes 147456 | tf_op jit(solution)/shard_map/reduce_scatter | solution.py:52
  356.0 65.9 %copy-start.6 = (bf16[3,32]{1,0:T(4,128)(2,1)S(1)}, bf16[3,32]{1,0:T(4,128)(2,1)}, u32[]{:S(2)}) copy-start(bf16[3,32]{1,0:T(4,128)(2,1)} %param.19) | copy-start | bytes 580
  356.0 65.9 %copy-start.2 = (bf16[1024,128]{1,0:T(8,128)(2,1)S(1)}, bf16[1024,128]{1,0:T(8,128)(2,1)}, u32[]{:S(2)}) copy-start(bf16[1024,128]{1,0:T(8,128)(2,1)} %param.13) | copy-start | bytes 786436
  356.0 66.1 %copy-start.7 = (bf16[1024]{0:T(1024)(128)(2,1)S(1)}, bf16[1024]{0:T(1024)(128)(2,1)}, u32[]{:S(2)}) copy-start(bf16[1024]{0:T(1024)(128)(2,1)} %param.14) | copy-start | bytes 6148
  356.0 9.9 %collective-permute-start.20 = (f32[512,128]{0,1:T(8,128)S(1)}, f32[512,128]{0,1:T(8,128)S(1)}, u32[]{:S(2)}, u32[]{:S(2)}) collective-permute-start(f32[512,128]{0,1:T(8,128)S(1)} %slice_select_fusion.2), channel_id=1, source_target_pairs={{0,16},{16,0},{8,24},{24,8},{32,48},{48,32},{40,56},{56,40},{64,80... | collective-permute-start | bytes 786440 | tf_op jit(solution)/shard_map/ppermute | solution.py:16
  366.0 6.9 %collective-permute-start.21 = (f32[256,128]{0,1:T(8,128)S(1)}, f32[256,128]{0,1:T(8,128)S(1)}, u32[]{:S(2)}, u32[]{:S(2)}) collective-permute-start(f32[256,128]{0,1:T(8,128)S(1)} %slice_select_fusion.8), channel_id=1, source_target_pairs={{0,8},{8,0},{16,24},{24,16},{32,40},{40,32},{48,56},{56,48},{64,72... | collective-permute-start | bytes 393224 | tf_op jit(solution)/shard_map/ppermute | solution.py:16
  373.7 85.5 %reduce-scatter.27.cloned.1.call-start = ((), (), s32[]{:S(2)}) async-start(), calls=%async_computation.16 | async-start | bytes 147456
  414.2 6.9 %collective-permute-start.22 = (f32[256,128]{0,1:T(8,128)S(1)}, f32[256,128]{0,1:T(8,128)S(1)}, u32[]{:S(2)}, u32[]{:S(2)}) collective-permute-start(f32[256,128]{0,1:T(8,128)S(1)} %slice_select_fusion.7), channel_id=1, source_target_pairs={{0,8},{8,0},{16,24},{24,16},{32,40},{40,32},{48,56},{56,48},{64,72... | collective-permute-start | bytes 393224 | tf_op jit(solution)/shard_map/ppermute | solution.py:16
  421.8 83.6 %reduce-scatter.29.cloned.1.call-start = ((), (), s32[]{:S(2)}) async-start(), calls=%async_computation.17 | async-start | bytes 147456
  460.2 6.9 %collective-permute-start.23 = (f32[256,128]{0,1:T(8,128)S(1)}, f32[256,128]{0,1:T(8,128)S(1)}, u32[]{:S(2)}, u32[]{:S(2)}) collective-permute-start(f32[256,128]{0,1:T(8,128)S(1)} %slice_select_fusion.6), channel_id=1, source_target_pairs={{0,8},{8,0},{16,24},{24,16},{32,40},{40,32},{48,56},{56,48},{64,72... | collective-permute-start | bytes 393224 | tf_op jit(solution)/shard_map/ppermute | solution.py:16
Sparse Core Ops, SparseCore 0:
  183.1 40.2 reduce-scatter.18
  255.4 41.4 reduce-scatter.20
  315.7 39.1 reduce-scatter.22
  373.8 39.3 reduce-scatter.24
  421.9 37.1 reduce-scatter.26
  468.0 37.4 reduce-scatter.28
